TPU v7x, 256 devices: a whole 4x4x8 slice. The times are simulated.
256 devices in a mesh: var: 4 (over x), tok: 2 (over z_hi), mp: 32 (over z_lo, y, core).
Axes of the slice: x: 4, y: 4, z: 8 (z_hi: 2, z_lo: 4; z = z_hi * 4 + z_lo), core: 2. Of those that a mesh axis runs over, the one named last changes fastest.
Arguments:
- patches: bfloat16 [88, 32, 64], P('var', 'tok'), may hold values from -6 to 6
- embed_weight: bfloat16 [88, 64, 12288], P('var', None, 'mp'), may hold values from -0.75 to 0.75
- embed_bias: bfloat16 [88, 12288], P('var', 'mp'), may hold values from -3 to 3
- queries: bfloat16 [32, 12288], P('tok', 'mp'), may hold values from -6 to 6
- score_bias: float32 [32, 88], P('tok'), may hold values from -4 to 260
- key_weight: bfloat16 [32, 384, 12288], P(None, 'var', 'mp'), may hold values from -0.0546875 to 0.0546875
- value_weight: bfloat16 [32, 384, 12288], P(None, 'var', 'mp'), may hold values from -0.0546875 to 0.0546875
- out_weight: bfloat16 [12288, 12288], P('mp', 'var'), may hold values from -0.109375 to 0.109375
- out_bias: bfloat16 [12288], P(('var', 'mp')), may hold values from -3 to 3
Outputs:
- aggregated: bfloat16 [32, 12288], P('tok', ('var', 'mp'))
All inputs are finite; a program needn't handle non-finite values.
Results may differ from a plain program's by a relative error of at most 0.005.
Values may be sent and summed in bfloat16 or wider, within the bound.
No kernel may reach another device: no remote copies, remote signals or barrier semaphores. Data moves between devices by JAX's collectives and lax.ppermute only.
A program may use at most 128 MiB of HBM per device.

v0:
```python
import math

import jax
import jax.numpy as jnp
from jax import lax
from jax.sharding import PartitionSpec as P

HD = 384


def on_device(
    patches,
    embed_weight,
    embed_bias,
    queries,
    score_bias,
    key_weight,
    value_weight,
    out_weight,
    out_bias,
):
    var_count = lax.axis_size("var")
    var_place = lax.axis_index("var")
    embedded = jnp.einsum("vtp,vpc->vtc", patches, embed_weight, preferred_element_type=jnp.float32)
    embedded = (embedded + embed_bias[:, None, :].astype(jnp.float32)).astype(jnp.bfloat16)
    local_vars, tok_rows, tile_width = embedded.shape
    quarter = tile_width // var_count
    tile_count = key_weight.shape[0]
    all_vars = local_vars * var_count
    gathered = lax.all_gather(embedded, "mp", axis=2, tiled=True)
    split_parts = gathered.reshape(local_vars, tok_rows, tile_count, var_count, quarter)
    received = lax.all_to_all(split_parts, "var", split_axis=3, concat_axis=0, tiled=True)
    received = received.reshape(all_vars, tok_rows, tile_count, quarter)
    key_part = jnp.einsum("vtkq,kqc->vtc", received, key_weight, preferred_element_type=jnp.float32)
    value_part = jnp.einsum(
        "vtkq,kqc->vtc", received, value_weight, preferred_element_type=jnp.float32
    )
    key_total, value_total = (
        lax.psum_scatter(key_part, "var", scatter_dimension=1, tiled=True),
        lax.psum_scatter(value_part, "var", scatter_dimension=1, tiled=True),
    )
    part_tokens = tok_rows // var_count
    heads_here = tile_width // HD
    key_heads = key_total.reshape(all_vars, part_tokens, heads_here, HD)
    value_heads = value_total.reshape(all_vars, part_tokens, heads_here, HD)
    key_normed = key_heads * lax.rsqrt(
        jnp.mean(key_heads * key_heads, axis=-1, keepdims=True) + 1e-06
    )
    query_rows = lax.dynamic_slice_in_dim(queries, var_place * part_tokens, part_tokens, 0)
    query_heads = query_rows.astype(jnp.float32).reshape(part_tokens, heads_here, HD)
    bias_rows = lax.dynamic_slice_in_dim(score_bias, var_place * part_tokens, part_tokens, 0)
    scores = jnp.einsum(
        "thd,vthd->thv", query_heads, key_normed, precision=lax.Precision.HIGHEST
    ) / math.sqrt(HD)
    scores = scores + bias_rows[:, None, :]
    attention = jax.nn.softmax(scores, axis=-1)
    mixed = jnp.einsum("thv,vthd->thd", attention, value_heads, precision=lax.Precision.HIGHEST)
    mixed = mixed.astype(jnp.bfloat16).reshape(part_tokens, tile_width)
    every_token = lax.all_gather(mixed, "var", axis=0, tiled=True)
    summed = lax.psum_scatter(
        lax.dot_general(
            out_weight, every_token, (((0,), (1,)), ((), ())), preferred_element_type=jnp.float32
        ),
        "mp",
        scatter_dimension=0,
        tiled=True,
    )
    return (summed.T + out_bias.astype(jnp.float32)[None, :]).astype(jnp.bfloat16)


def solution(mesh):
    in_specs = (
        P("var", "tok", None),
        P("var", None, "mp"),
        P("var", "mp"),
        P("tok", "mp"),
        P("tok", None),
        P(None, "var", "mp"),
        P(None, "var", "mp"),
        P("mp", "var"),
        P(("var", "mp")),
    )
    out_specs = P("tok", ("var", "mp"))
    return jax.shard_map(
        on_device, mesh=mesh, in_specs=in_specs, out_specs=out_specs, check_vma=False
    )
```

profile of v0, /device:TPU:1, one launch (start us, length us, event | category | flops | bytes accessed | tf_op | source)
XLA Modules:
  0.0 487.0 jit_solution(4182430906683709415)
XLA Ops:
  6.5 0.9 convert_element_type.21
  7.4 2.3 fusion.7
  9.7 0.0 all-gather.3.cloned.1.call-update
  9.7 0.0 reduce-scatter.6.cloned.1.call-start
  9.8 75.2 %all-gather.3.cloned.1.call-done = bf16[22,16,12288]{2,1,0:T(8,128)(2,1)} async-done(((bf16[22,16,384]{2,1,0:T(8,128)(2,1)}), bf16[22,16,12288]{2,1,0:T(8,128)(2,1)}) %all-gather.3.cloned.1.call-update) | async-done | bytes 8650768 | tf_op jit(solution)/shard_map/all_gather | solution.py:30
  85.0 20.5 %reshape.56 = bf16[22,16,32,4,96]{4,3,2,1,0:T(4,128)(2,1)} reshape(bf16[22,16,12288]{2,1,0:T(8,128)(2,1)} %all-gather.3.cloned.1.call-done) | data formatting | bytes 17301504 | tf_op jit(solution)/shard_map/reshape | solution.py:31
  105.5 7.1 %copy.11 = bf16[22,16,32,4,96]{4,2,1,0,3:T(8,128)(2,1)S(1)} copy(bf16[22,16,32,4,96]{4,3,2,1,0:T(4,128)(2,1)} %reshape.56) | data formatting | bytes 17301504 | tf_op jit(solution)/shard_map/reshape | solution.py:31
  112.6 130.9 %all_to_all.15 = bf16[22,16,32,4,96]{4,2,1,0,3:T(8,128)(2,1)S(1)} all-to-all(bf16[22,16,32,4,96]{4,2,1,0,3:T(8,128)(2,1)S(1)} %copy.11), channel_id=1, replica_groups=mesh['var'=4,'tok'=2,'mp'=32] {'var'}, dimensions={3} | all-to-all | bytes 17301504 | tf_op jit(solution)/shard_map/all_to_all | solution.py:32
  243.5 4.9 %copy.12 = bf16[4,22,16,32,1,96]{5,2,3,1,0,4:T(8,128)(2,1)S(1)} copy(bf16[4,22,16,32,1,96]{5,3,2,1,0,4:T(8,128)(2,1)S(1)} %bitcast.46) | data formatting | bytes 17301504 | tf_op jit(solution)/shard_map/all_to_all | solution.py:32
  248.5 4.7 fusion.4
  253.2 2.1 copy.13
  255.3 0.0 reduce-scatter.6.cloned.1.call-update
  255.3 0.0 reduce-scatter.8.cloned.1.call-start
  255.4 8.3 %fusion = f32[88,16,384,1]{2,1,3,0:T(8,128)S(1)} fusion(bf16[88,16,32,96]{3,1,2,0:T(8,128)(2,1)} %bitcast.48, bf16[32,96,384]{2,1,0:T(8,128)(2,1)} %param.15), kind=kOutput, calls=%fused_computation.1 | convolution fusion | flops 3321888768 | bytes 13172736 | tf_op jit(solution)/shard_map/vtkq,kqc->vtc/dot_general | solution.py:35
  263.7 2.0 copy.28
  265.7 0.0 reduce-scatter.10.cloned.1.call-start
  265.8 0.7 dynamic-slice_bitcast_fusion
  266.5 19.5 %reduce-scatter.6.cloned.1.call-done = f32[88,4,384]{2,0,1:T(8,128)} async-done(((f32[88,16,384]{2,0,1:T(8,128)}), f32[88,4,384]{2,0,1:T(8,128)}) %reduce-scatter.6.cloned.1.call-update) | async-done | bytes 540688 | tf_op jit(solution)/shard_map/reduce_scatter | solution.py:39
  285.9 1.2 multiply_reduce_fusion
  287.1 1.5 fusion.8
  288.7 0.8 fusion.16
  289.5 0.2 fusion.15
  289.7 0.1 fusion.14
  289.7 31.5 %reduce-scatter.8.cloned.1.call-done = f32[88,4,384]{2,0,1:T(8,128)} async-done(((f32[88,16,384]{2,0,1:T(8,128)}), f32[88,4,384]{2,0,1:T(8,128)}) %reduce-scatter.8.cloned.1.call-update) | async-done | bytes 540688 | tf_op jit(solution)/shard_map/reduce_scatter | solution.py:40
  321.3 1.5 fusion.17
  322.7 9.0 %all-gather = bf16[4,4,384]{2,1,0:T(4,128)(2,1)S(1)} all-gather(bf16[1,4,384]{2,1,0:T(4,128)(2,1)S(1)} %bitcast.50), channel_id=1, replica_groups=mesh['var'=4,'tok'=2,'mp'=32] {'var'}, dimensions={0}, use_global_device_ids=true | all-gather | bytes 15360 | tf_op jit(solution)/shard_map/all_gather | solution.py:59
  331.7 2.2 convolution_bitcast_fusion
  334.0 1.6 copy.20
  335.6 0.0 reduce-scatter.10.cloned.1.call-update
  335.6 143.4 %reduce-scatter.10.cloned.1.call-done = f32[96,16]{1,0:T(8,128)} async-done(((f32[3072,16]{1,0:T(8,128)}), f32[96,16]{1,0:T(8,128)}) %reduce-scatter.10.cloned.1.call-update) | async-done | bytes 6160
  479.0 0.9 copy.21
  479.8 0.6 fusion.12
  (14 shorter events, 0.1 us)
Async XLA Ops:
  6.5 241.9 %copy-start = (bf16[32,96,384]{2,1,0:T(8,128)(2,1)S(1)}, bf16[32,96,384]{2,1,0:T(8,128)(2,1)}, u32[]{:S(2)}) copy-start(bf16[32,96,384]{2,1,0:T(8,128)(2,1)} %param.14) | copy-start | bytes 7077892
  6.5 78.5 %all-gather.3.cloned.1.call-start = ((), (), s32[]{:S(2)}) async-start(), calls=%async_computation.4 | async-start | bytes 8921088 | tf_op jit(solution)/shard_map/all_gather | solution.py:30
  9.7 276.2 %reduce-scatter.6.cloned.1.call-start = ((), (), s32[]{:S(2)}) async-start(), calls=%async_computation.5 | async-start | bytes 2703360 | tf_op jit(solution)/shard_map/reduce_scatter | solution.py:39
  248.4 4.7 copy-start.2
  255.3 65.9 %reduce-scatter.8.cloned.1.call-start = ((), (), s32[]{:S(2)}) async-start(), calls=%async_computation.6 | async-start | bytes 2703360 | tf_op jit(solution)/shard_map/reduce_scatter | solution.py:40
  265.7 213.3 %reduce-scatter.10.cloned.1.call-start = ((), (), s32[]{:S(2)}) async-start(), calls=%async_computation.7 | async-start | bytes 1622016
  331.7 148.8 %copy-start.1 = (bf16[32,96,384]{2,1,0:T(8,128)(2,1)S(1)}, bf16[32,96,384]{2,1,0:T(8,128)(2,1)}, u32[]{:S(2)}) copy-start(bf16[32,96,384]{2,1,0:T(8,128)(2,1)} %param.14) | copy-start | bytes 7077892
  331.7 3.9 copy-start.3
Sparse Core Ops, SparseCore 0:
  9.9 75.1 all-gather.2
  255.4 30.4 reduce-scatter.5
  288.6 32.5 reduce-scatter.7
  335.7 143.2 reduce-scatter.9
where the time goes:
time: 492 us; the launch traced here: 487 us
  waiting for transfers between devices  270 us (55%)
  blocking collectives  140 us (28%)
  local copies, waits for them, and re-layouts  39.9 us (8%)
  matrix products  20.5 us (4%)
  between operations  13.2 us (3%)
    unnamed x5, waiting for transfers between devices  143 us
    all_to_all x1, blocking collectives, on_device(): lax.all_to_all(split_parts, 'var', split_axis=3, concat_axis=0, tiled=True)  131 us
    all_gather x1, waiting for transfers between devices, on_device(): gathered = lax.all_gather(embedded, 'mp', axis=2, tiled=True)  75.2 us
    reduce_scatter x1, waiting for transfers between devices, on_device(): lax.psum_scatter(value_part, 'var', scatter_dimension=1, tiled=True)  31.5 us
    reshape x2, local copies, waits for them, and re-layouts, on_device(): gathered.reshape(local_vars, tok_rows, tile_count, var_count, quarter)  27.6 us
    reduce_scatter x1, waiting for transfers between devices, on_device(): lax.psum_scatter(key_part, 'var', scatter_dimension=1, tiled=True)  19.5 us
  transfers between devices with their start and end apart: 4, of which 4 were waited for; matrix products, arithmetic and copies ran while one was open for 3% of the time, Pallas kernels for 0%

commit v1 on v0

v1 whole, which is shorter than its diff:
```python
import math

import jax
import jax.numpy as jnp
from jax import lax
from jax.sharding import PartitionSpec as P

HD = 384


def on_device(
    patches,
    embed_weight,
    embed_bias,
    queries,
    score_bias,
    key_weight,
    value_weight,
    out_weight,
    out_bias,
):
    var_count = lax.axis_size("var")
    mp_count = lax.axis_size("mp")
    var_place = lax.axis_index("var")
    local_vars, tok_rows, _ = patches.shape
    all_vars = local_vars * var_count
    tile_width = embed_weight.shape[2]
    quarter = tile_width // var_count
    part_tokens = tok_rows // var_count
    embedded = jnp.einsum("vpc,vtp->vct", embed_weight, patches, preferred_element_type=jnp.float32)
    embedded = (embedded + embed_bias[:, :, None].astype(jnp.float32)).astype(jnp.bfloat16)
    own = embedded.transpose(1, 2, 0).reshape(var_count, quarter, tok_rows, local_vars)
    received = lax.all_to_all(own, "var", split_axis=0, concat_axis=3, tiled=True)
    block = received.reshape(quarter, tok_rows * all_vars)
    gathered = lax.all_gather(block, "mp", axis=0, tiled=True)
    features = mp_count * quarter
    key_part = lax.dot_general(
        key_weight.reshape(features, tile_width), gathered, (((0,), (0,)), ((), ())),
        preferred_element_type=jnp.float32,
    ).astype(jnp.bfloat16)
    value_part = lax.dot_general(
        value_weight.reshape(features, tile_width), gathered, (((0,), (0,)), ((), ())),
        preferred_element_type=jnp.float32,
    ).astype(jnp.bfloat16)
    parts = jnp.stack([key_part, value_part]).reshape(
        2, tile_width, var_count, part_tokens * all_vars
    ).transpose(2, 0, 1, 3)
    parts = lax.all_to_all(parts, "var", split_axis=0, concat_axis=0, tiled=True)
    totals = parts.astype(jnp.float32).sum(0)
    heads_here = tile_width // HD
    totals = totals.reshape(2, heads_here, HD, part_tokens, all_vars)
    keys, values = totals[0], totals[1]
    scale = lax.rsqrt(jnp.mean(keys * keys, axis=1) + 1e-06)
    query_rows = lax.dynamic_slice_in_dim(queries, var_place * part_tokens, part_tokens, 0)
    query_heads = query_rows.astype(jnp.float32).reshape(part_tokens, heads_here, HD).transpose(1, 2, 0)
    bias_rows = lax.dynamic_slice_in_dim(score_bias, var_place * part_tokens, part_tokens, 0)
    scores = (query_heads[..., None] * keys).sum(1) * scale / math.sqrt(HD)
    attention = jax.nn.softmax(scores + bias_rows[None], axis=-1)
    mixed = (attention[:, None] * values).sum(-1).transpose(2, 0, 1)
    mixed = mixed.astype(jnp.bfloat16).reshape(part_tokens, tile_width)
    every_token = lax.all_gather(mixed, "var", axis=0, tiled=True)
    product = jnp.dot(every_token, out_weight, preferred_element_type=jnp.float32)
    product = product.astype(jnp.bfloat16).reshape(tok_rows, mp_count, -1).transpose(1, 0, 2)
    terms = lax.all_to_all(product, "mp", split_axis=0, concat_axis=0, tiled=True)
    summed = terms.astype(jnp.float32).sum(0)
    return (summed + out_bias.astype(jnp.float32)[None, :]).astype(jnp.bfloat16)


def solution(mesh):
    in_specs = (
        P("var", "tok", None),
        P("var", None, "mp"),
        P("var", "mp"),
        P("tok", "mp"),
        P("tok", None),
        P(None, "var", "mp"),
        P(None, "var", "mp"),
        P("mp", "var"),
        P(("var", "mp")),
    )
    out_specs = P("tok", ("var", "mp"))
    return jax.shard_map(
        on_device, mesh=mesh, in_specs=in_specs, out_specs=out_specs, check_vma=False
    )
```

time: 492 us -> 182 us (0.37)
  waiting for transfers between devices: 270 us -> 108 us
  blocking collectives: 140 us -> 20.5 us
  local copies, waits for them, and re-layouts: 39.9 us -> 2.41 us
  starting transfers between devices: 0.13 us -> 13.4 us
    unnamed x5 -> x1, waiting for transfers between devices: 143 us -> 0.02 us
    all_to_all x1, blocking collectives: 131 us -> 11.4 us  [on_device(): lax.all_to_all(own, 'var', split_axis=0, concat_axis=3, tiled=True)]
    reduce_scatter x2 -> x0, waiting for transfers between devices: 51 us -> none  [the longest x1 31.5 us: on_device(): lax.psum_scatter(value_part, 'var', scatter_dimension=1, tiled=True)]
    all_to_all x0 -> x2, waiting for transfers between devices: none -> 34.8 us  [the longest x1 26.2 us: on_device(): lax.all_to_all(parts, 'var', split_axis=0, concat_axis=0, tiled=True)]
    reshape x2 -> x6, local copies, waits for them, and re-layouts: 27.6 us -> 2.16 us  [the longest x2 1.02 us: on_device(): block = received.reshape(quarter, tok_rows * all_vars)]
    all_to_all x0 -> x2, starting transfers between devices: none -> 13.4 us  [the longest x1 9 us: on_device(): lax.all_to_all(product, 'mp', split_axis=0, concat_axis=0, tiled=True)]
    dot_general x6 -> x4, matrix products: 20.5 us -> 16.4 us  [the longest x1 8.07 us: on_device(): lax.dot_general(value_weight.reshape(features, tile_width), gathered, (((...]
  transfers between devices with their start and end apart: 4 -> 3, of which waited for: 4 -> 3; matrix products, arithmetic and copies ran while one was open for 3% -> 0% of each run, Pallas kernels for 0% -> 0%
where the time goes in v1:
time: 182 us; the launch traced here: 181 us
  waiting for transfers between devices  108 us (59%)
  blocking collectives  20.5 us (11%)
  matrix products  16.4 us (9%)
  between operations  13.5 us (7%)
  starting transfers between devices  13.4 us (7%)
  other arithmetic  7.26 us (4%)
  local copies, waits for them, and re-layouts  2.41 us (1%)
    all_gather x1, waiting for transfers between devices, on_device(): gathered = lax.all_gather(block, 'mp', axis=0, tiled=True)  72.8 us
    all_to_all x1, waiting for transfers between devices, on_device(): lax.all_to_all(parts, 'var', split_axis=0, concat_axis=0, tiled=True)  26.2 us
    all_to_all x1, blocking collectives, on_device(): lax.all_to_all(own, 'var', split_axis=0, concat_axis=3, tiled=True)  11.4 us
    all_gather x1, blocking collectives, on_device(): every_token = lax.all_gather(mixed, 'var', axis=0, tiled=True)  9.03 us
    all_to_all x1, starting transfers between devices, on_device(): lax.all_to_all(product, 'mp', split_axis=0, concat_axis=0, tiled=True)  9 us
    all_to_all x1, waiting for transfers between devices, on_device(): lax.all_to_all(product, 'mp', split_axis=0, concat_axis=0, tiled=True)  8.53 us
    dot_general x1, matrix products, on_device(): lax.dot_general(value_weight.reshape(features, tile_width), gathered, (((...  8.07 us
    dot_general x1, matrix products, on_device(): lax.dot_general(key_weight.reshape(features, tile_width), gathered, (((0,...  4.67 us
  transfers between devices with their start and end apart: 3, of which 3 were waited for; matrix products, arithmetic and copies ran while one was open for 0% of the time, Pallas kernels for 0%

profile of v1, /device:TPU:1, one launch (start us, length us, event | category | flops | bytes accessed | tf_op | source)
XLA Modules:
  0.0 181.1 jit_solution(18272130707966221392)
XLA Ops:
  6.5 0.0 copy-start
  6.5 0.9 convert_bitcast_fusion
  7.4 1.6 fusion.1
  9.0 0.2 reshape.106
  9.3 0.1 copy.19
  9.3 11.4 %all_to_all.25 = bf16[4,96,16,22]{1,2,3,0:T(8,128)(2,1)S(1)} all-to-all(bf16[4,96,16,22]{1,2,3,0:T(8,128)(2,1)S(1)} %copy.19), channel_id=1, replica_groups=mesh['var'=4,'tok'=2,'mp'=32] {'var'}, dimensions={0} | all-to-all | bytes 540672 | tf_op jit(solution)/shard_map/all_to_all | solution.py:33
  20.7 0.1 copy.20
  20.8 0.1 reshape.107
  21.0 0.9 copy.21
  21.9 0.0 all-gather.3.cloned.1.call-update
  21.9 72.8 %all-gather.3.cloned.1.call-done = bf16[3072,1408]{1,0:T(8,128)(2,1)} async-done(((bf16[96,1408]{1,0:T(8,128)(2,1)}), bf16[3072,1408]{1,0:T(8,128)(2,1)}) %all-gather.3.cloned.1.call-update) | async-done | bytes 8650768 | tf_op jit(solution)/shard_map/all_gather | solution.py:35
  94.7 8.1 %convolution_convert_fusion.1 = bf16[1408,384]{1,0:T(8,128)(2,1)S(1)} fusion(bf16[3072,1408]{1,0:T(8,128)(2,1)} %all-gather.3.cloned.1.call-done, bf16[3072,384]{1,0:T(8,128)(2,1)S(1)} %bitcast.56), kind=kOutput, calls=%fused_computation.2 | convolution fusion | flops 3322429440 | bytes 12091392 | tf_op jit(solution)/shard_map/dot_general | solution.py:41
  102.8 4.7 %convolution_convert_fusion.2 = bf16[1408,384]{1,0:T(8,128)(2,1)S(1)} fusion(bf16[3072,1408]{1,0:T(8,128)(2,1)S(1)} %copy-done.1, bf16[3072,384]{1,0:T(8,128)(2,1)S(1)} %bitcast.63), kind=kOutput, calls=%fused_computation.3 | convolution fusion | flops 3322429440 | bytes 12091392 | tf_op jit(solution)/shard_map/dot_general | solution.py:37
  107.5 1.6 maximum_bitcast_fusion
  109.0 4.4 %all-to-all-start.1 = ((bf16[4,2,384,352]{2,3,1,0:T(8,128)(2,1)}), bf16[4,2,384,352]{2,3,1,0:T(8,128)(2,1)}, u32[]{:S(2)}, u32[]{:S(2)}) async-start(bf16[4,2,384,352]{2,3,1,0:T(8,128)(2,1)} %maximum_bitcast_fusion), calls=%async_computation.1 | async-start | bytes 4325376 | tf_op jit(solution)/shard_map/all_to_all | solution.py:48
  113.5 0.7 convert_bitcast_fusion.1
  114.2 26.2 %all-to-all-done.1 = bf16[4,2,384,352]{2,3,1,0:T(8,128)(2,1)} async-done(((bf16[4,2,384,352]{2,3,1,0:T(8,128)(2,1)}), bf16[4,2,384,352]{2,3,1,0:T(8,128)(2,1)}, u32[]{:S(2)}, u32[]{:S(2)}) %all-to-all-start.1) | async-done | bytes 2162720 | tf_op jit(solution)/shard_map/all_to_all | solution.py:48
  140.4 2.0 %convert_reduce_fusion = f32[2,384,352]{1,2,0:T(8,128)S(1)} fusion(bf16[4,2,384,352]{2,3,1,0:T(8,128)(2,1)} %all-to-all-done.1), kind=kLoop, calls=%fused_computation | loop fusion | flops 1892352 | bytes 3244032 | tf_op jit(solution)/shard_map/reduce_sum | solution.py:49
  142.5 0.2 multiply_reduce_fusion.1
  142.7 0.0 copy-start.3
  142.7 0.1 reshape.114
  142.8 0.8 fusion.6
  143.6 0.2 fusion.5
  143.8 0.1 fusion.4
  143.9 0.2 multiply_reduce_fusion
  144.1 9.0 %all-gather = bf16[16,1,384]{2,1,0:T(2,128)(2,1)S(1)} all-gather(bf16[4,1,384]{2,1,0:T(2,128)(2,1)S(1)} %copy.24), channel_id=2, replica_groups=mesh['var'=4,'tok'=2,'mp'=32] {'var'}, dimensions={0}, use_global_device_ids=true | all-gather | bytes 15360 | tf_op jit(solution)/shard_map/all_gather | solution.py:61
  153.1 2.1 %convolution_convert_fusion = bf16[16,3072]{1,0:T(8,128)(2,1)S(1)} fusion(bf16[384,3072]{1,0:T(8,128)(2,1)} %param.16, bf16[16,1,384]{2,1,0:T(2,128)(2,1)S(1)} %all-gather), kind=kOutput, calls=%fused_computation.1 | convolution fusion | flops 37797888 | bytes 2469888 | tf_op jit(solution)/shard_map/dot_general | solution.py:62
  155.2 0.2 reshape.111
  155.3 0.7 copy.32
  156.0 9.0 %all-to-all-start.2 = ((bf16[32,16,96]{2,1,0:T(8,128)(2,1)}), bf16[32,16,96]{2,1,0:T(8,128)(2,1)S(1)}, u32[]{:S(2)}, u32[]{:S(2)}) async-start(bf16[32,16,96]{2,1,0:T(8,128)(2,1)} %bitcast.55), calls=%async_computation.2 | async-start | bytes 262144 | tf_op jit(solution)/shard_map/all_to_all | solution.py:64
  165.1 8.5 %all-to-all-done.2 = bf16[32,16,96]{2,1,0:T(8,128)(2,1)S(1)} async-done(((bf16[32,16,96]{2,1,0:T(8,128)(2,1)}), bf16[32,16,96]{2,1,0:T(8,128)(2,1)S(1)}, u32[]{:S(2)}, u32[]{:S(2)}) %all-to-all-start.2) | async-done | bytes 98336 | tf_op jit(solution)/shard_map/all_to_all | solution.py:64
  173.6 0.6 add_convert_fusion
  (12 shorter events, 0.1 us)
Async XLA Ops:
  6.5 88.1 %copy-start = (bf16[32,96,384]{2,1,0:T(8,128)(2,1)S(1)}, bf16[32,96,384]{2,1,0:T(8,128)(2,1)}, u32[]{:S(2)}) copy-start(bf16[32,96,384]{2,1,0:T(8,128)(2,1)} %param.15) | copy-start | bytes 7077892
  6.5 88.1 %all-gather.3.cloned.1.call-start = ((), (), s32[]{:S(2)}) async-start(), calls=%async_computation.3 | async-start | bytes 8921088 | tf_op jit(solution)/shard_map/all_gather | solution.py:35
  94.7 8.1 %copy-start.1 = (bf16[3072,1408]{1,0:T(8,128)(2,1)S(1)}, bf16[3072,1408]{1,0:T(8,128)(2,1)}, u32[]{:S(2)}) copy-start(bf16[3072,1408]{1,0:T(8,128)(2,1)} %all-gather.3.cloned.1.call-done) | copy-start | bytes 25952260
  94.7 8.1 %copy-start.2 = (bf16[32,96,384]{2,1,0:T(8,128)(2,1)S(1)}, bf16[32,96,384]{2,1,0:T(8,128)(2,1)}, u32[]{:S(2)}) copy-start(bf16[32,96,384]{2,1,0:T(8,128)(2,1)} %param.14) | copy-start | bytes 7077892
  109.0 31.4 %all-to-all-start.1 = ((bf16[4,2,384,352]{2,3,1,0:T(8,128)(2,1)}), bf16[4,2,384,352]{2,3,1,0:T(8,128)(2,1)}, u32[]{:S(2)}, u32[]{:S(2)}) async-start(bf16[4,2,384,352]{2,3,1,0:T(8,128)(2,1)} %maximum_bitcast_fusion), calls=%async_computation.1 | async-start | bytes 4325376 | tf_op jit(solution)/shard_map/all_to_all | solution.py:48
  142.7 22.3 %copy-start.3 = (bf16[96]{0:T(256)(128)(2,1)S(1)}, bf16[96]{0:T(256)(128)(2,1)}, u32[]{:S(2)}) copy-start(bf16[96]{0:T(256)(128)(2,1)} %param.17) | copy-start | bytes 580
  156.0 17.6 %all-to-all-start.2 = ((bf16[32,16,96]{2,1,0:T(8,128)(2,1)}), bf16[32,16,96]{2,1,0:T(8,128)(2,1)S(1)}, u32[]{:S(2)}, u32[]{:S(2)}) async-start(bf16[32,16,96]{2,1,0:T(8,128)(2,1)} %bitcast.55), calls=%async_computation.2 | async-start | bytes 262144 | tf_op jit(solution)/shard_map/all_to_all | solution.py:64
Sparse Core Ops, SparseCore 0:
  22.0 72.6 all-gather.2

commit v2 on v1

v2 whole, which is shorter than its diff:
```python
import functools
import math

import jax
import jax.numpy as jnp
import numpy as np
from jax import lax
from jax.experimental import pallas as pl
from jax.experimental.pallas import tpu as pltpu
from jax.sharding import PartitionSpec as P

HD = 384
Z, Y, C = 4, 4, 2
STEPS = (2, 1, 3, 0)
COST = 2**16
VMEM = 8 * 2**20


def move(array, there):
    pairs = []
    for z in range(Z):
        for y in range(Y):
            for c in range(C):
                z2, y2, c2 = there(z, y, c)
                pairs.append(((z * Y + y) * C + c, ((z2 % Z) * Y + y2 % Y) * C + c2 % C))
    return lax.ppermute(array, "mp", pairs)


def other_core(array):
    return move(array, lambda z, y, c: (z, y, 1 - c))


def along_z(array, step):
    return move(array, lambda z, y, c: (z + step, y, c))


def along_y(array):
    return move(array, lambda z, y, c: (z, y + 1 - 2 * c, c))


def local_call(kernel, after, arrays, specs, out_shape, out_block, name, aliases=None):
    return pl.pallas_call(
        kernel,
        grid=(1,),
        in_specs=[pl.BlockSpec(memory_space=pl.ANY)] + specs,
        out_specs=out_block,
        out_shape=jax.ShapeDtypeStruct(out_shape, jnp.bfloat16),
        input_output_aliases=aliases or {},
        compiler_params=pltpu.CompilerParams(vmem_limit_bytes=VMEM),
        cost_estimate=pl.CostEstimate(flops=0, transcendentals=0, bytes_accessed=COST),
        name=name,
    )(after, *arrays)


def copy_kernel(after, array, out):
    out[...] = array[...]


def pack_kernel(after, received, out):
    owners, groups, _, width = received.shape
    for group in range(groups):
        for owner in range(owners):
            out[group, :, owner * width : (owner + 1) * width] = received[owner, group]


def pack(received, after):
    owners, groups, rows, width = received.shape
    shape = (groups, rows, owners * width)
    return local_call(
        pack_kernel,
        after,
        [received],
        [pl.BlockSpec(received.shape, lambda k: (0, 0, 0, 0))],
        shape,
        pl.BlockSpec(shape, lambda k: (0, 0, 0)),
        "pack",
    )


def first_half(array, after):
    rows, width = array.shape
    block = pl.BlockSpec((rows, width // 2), lambda k: (0, 0))
    return local_call(copy_kernel, after, [array], [block], (rows, width // 2), block, "half")


def line_kernel(chunk, groups, after, *refs):
    *parts, out, wide = refs
    tile = out.shape[1] // len(parts)
    rows = parts[0].shape[1]
    for n, part in enumerate(parts):
        values = part[groups[chunk]].astype(jnp.float32)
        for block in range(values.shape[1] // tile):
            wide[block * rows : (block + 1) * rows, n * tile : (n + 1) * tile] = values[
                :, block * tile : (block + 1) * tile
            ]
    out[...] = wide[...].astype(out.dtype)


def line_of(parts, chunk, groups, after):
    _, rows, width = parts[0].shape
    tile = width // 4
    shape = (rows * 4, tile * len(parts))
    return pl.pallas_call(
        functools.partial(line_kernel, chunk),
        in_specs=[pl.BlockSpec(memory_space=pltpu.SMEM), pl.BlockSpec(memory_space=pl.ANY)]
        + [pl.BlockSpec(memory_space=pltpu.VMEM) for _ in parts],
        out_specs=pl.BlockSpec(memory_space=pltpu.VMEM),
        out_shape=jax.ShapeDtypeStruct(shape, jnp.bfloat16),
        scratch_shapes=[pltpu.VMEM(shape, jnp.float32)],
        compiler_params=pltpu.CompilerParams(vmem_limit_bytes=VMEM),
        cost_estimate=pl.CostEstimate(flops=0, transcendentals=0, bytes_accessed=COST),
        name="line",
    )(groups, after, *parts)


def order_kernel(order, keys, values, *refs):
    count = len(refs) - 3
    outs, (held, sems, out_sems) = refs[:count], refs[count:]
    width = keys.shape[2]
    copies, leaving = [], []
    for n in range(keys.shape[0]):
        for k, weight in enumerate((keys, values)):
            copy = pltpu.make_async_copy(
                weight.at[order[n]], held.at[n, :, pl.ds(k * width, width)], sems.at[k, n]
            )
            copy.start()
            copies.append(copy)
    first = 0
    for m, out in enumerate(outs):
        last = first + out.shape[0]
        for copy in copies[2 * first : 2 * last]:
            copy.wait()
        leaving.append(
            pltpu.make_async_copy(held.at[pl.ds(first, last - first)], out, out_sems.at[m])
        )
        leaving[-1].start()
        first = last
    for copy in leaving:
        copy.wait()


def ordered_weights(order, keys, values, counts):
    tiles, rows, width = keys.shape
    anywhere = pl.BlockSpec(memory_space=pl.ANY)
    return pl.pallas_call(
        order_kernel,
        in_specs=[pl.BlockSpec(memory_space=pltpu.SMEM), anywhere, anywhere],
        out_specs=[pl.BlockSpec(memory_space=pltpu.HBM) for _ in counts],
        out_shape=[pltpu.HBM((n, rows, 2 * width), keys.dtype) for n in counts],
        scratch_shapes=[
            pltpu.VMEM((tiles, rows, 2 * width), keys.dtype),
            pltpu.SemaphoreType.DMA((2, tiles)),
            pltpu.SemaphoreType.DMA((len(counts),)),
        ],
        compiler_params=pltpu.CompilerParams(vmem_limit_bytes=VMEM),
        cost_estimate=pl.CostEstimate(flops=0, transcendentals=0, bytes_accessed=10 * 2**20),
        name="order_weights",
    )(order, keys, values)


def arrival_order(ids):
    def sent(ids, there):
        result = np.zeros_like(ids)
        for n in range(Z * Y * C):
            z, y, c = there(n // (Y * C), n // C % Y, n % C)
            result[(z % Z * Y + y % Y) * C + c % C] = ids[n]
        return result

    def up_or_down(ids):
        return sent(ids, lambda z, y, c: (z, y + 1 - 2 * c, c))

    def swapped(ids):
        return sent(ids, lambda z, y, c: (z, y, 1 - c))

    mine = [ids] + [sent(ids, lambda z, y, c: (z + step, y, c)) for step in (1, 3, 2)]
    line = np.concatenate(mine + [swapped(part) for part in mine], axis=1)
    near = up_or_down(line)
    far = up_or_down(near[:, : near.shape[1] // 2])
    return np.concatenate([line, near, swapped(near), far, swapped(far)], axis=1)


def core_var_shift(array):
    n = lax.axis_size("var")
    m = lax.axis_size("mp")
    pairs = [
        (k * m + p, (k + 1 - 2 * (p % C)) % n * m + p) for k in range(n) for p in range(m)
    ]
    return lax.ppermute(array, ("var", "mp"), pairs)


def var_shift(array, step):
    n = lax.axis_size("var")
    return lax.ppermute(array, "var", [(k, (k + step) % n) for k in range(n)])


def on_device(
    patches,
    embed_weight,
    embed_bias,
    queries,
    score_bias,
    key_weight,
    value_weight,
    out_weight,
    out_bias,
):
    var_count = lax.axis_size("var")
    mp_count = lax.axis_size("mp")
    var_place = lax.axis_index("var")
    local_vars, tok_rows, _ = patches.shape
    all_vars = local_vars * var_count
    tile_width = embed_weight.shape[2]
    quarter = tile_width // var_count
    part_tokens = tok_rows // var_count
    rows = part_tokens * all_vars
    f32 = jnp.float32
    embedded = jnp.einsum("vtp,vpc->vtc", patches, embed_weight, preferred_element_type=f32)
    embedded = (embedded + embed_bias[:, None, :].astype(f32)).astype(jnp.bfloat16)
    own = embedded.reshape(local_vars, var_count, part_tokens, var_count, quarter)
    own = own.transpose(3, 1, 0, 2, 4).reshape(var_count, var_count, -1, quarter)
    order = arrival_order(np.arange(mp_count)[:, None])
    order = jnp.take(jnp.asarray(order, jnp.int32), lax.axis_index("mp"), axis=0)
    weights = ordered_weights(order, key_weight, value_weight, (8, 8, 8, 4, 4))
    received = lax.all_to_all(own, "var", split_axis=0, concat_axis=0, tiled=True)
    tiles = pack(received, weights[0])
    weights = [w.reshape(-1, 2 * tile_width) for w in weights]
    tiles = [tiles] + [along_z(tiles, step) for step in (1, 3, 2)]
    tiles += [other_core(part) for part in tiles]
    groups = jnp.stack([(var_place + step) % var_count for step in STEPS]).astype(jnp.int32)

    def line(chunk, after):
        return line_of(tiles, chunk, groups, after)

    def product(line, near, half):
        far = along_y(half)
        parts = [line, near, other_core(near), far, other_core(far)]
        total = 0.0
        for part, weight in zip(parts, weights):
            total = total + jnp.dot(part, weight, preferred_element_type=f32)
        return total

    core = lax.axis_index("mp") % C
    line0 = line(0, out_bias)
    near0 = along_y(line0)
    line1 = line(1, line0)
    near1 = along_y(line1)
    half0 = first_half(near0, line1)
    line2 = line(2, half0)
    near2 = along_y(line2)
    line3 = line(3, line2)
    near3 = along_y(line3)
    far_sent = product(line0, near0, half0).astype(jnp.bfloat16)
    far = core_var_shift(far_sent).astype(f32)
    half1 = first_half(near1, far_sent)
    half2 = first_half(near2, half1)
    ahead = product(line1, near1, half1)
    ahead_sent = (ahead + jnp.where(core == 0, far, 0.0)).astype(jnp.bfloat16)
    half3 = first_half(near3, ahead_sent)
    behind = product(line2, near2, half2)
    from_behind = var_shift(ahead_sent, 1)
    from_ahead = var_shift((behind + jnp.where(core == 1, far, 0.0)).astype(jnp.bfloat16), -1)
    totals = product(line3, near3, half3)
    totals = totals + from_behind.astype(f32) + from_ahead.astype(f32)

    keys, values = totals[:, :tile_width], totals[:, tile_width:]
    scale = lax.rsqrt(jnp.mean(keys * keys, axis=1) + 1e-06)
    query_rows = lax.dynamic_slice_in_dim(queries, var_place * part_tokens, part_tokens, 0)
    bias_rows = lax.dynamic_slice_in_dim(score_bias, var_place * part_tokens, part_tokens, 0)
    token = np.arange(rows) % part_tokens
    spot = jnp.asarray(token[:, None] == np.arange(part_tokens))
    spread = jnp.dot(spot.astype(jnp.bfloat16), query_rows, preferred_element_type=f32)
    scores = (spread * keys).sum(1) * scale / math.sqrt(HD) + bias_rows.T.reshape(rows)
    scores = jnp.where(spot, scores[:, None], -jnp.inf)
    weight = jnp.exp(scores - scores.max(0, keepdims=True))
    attention = weight / weight.sum(0, keepdims=True)
    mixed = lax.dot_general(
        attention, values, (((0,), (0,)), ((), ())), precision=lax.Precision.HIGHEST
    ).astype(jnp.bfloat16)

    every_token = jnp.zeros((tok_rows, tile_width), jnp.bfloat16)
    for step in range(var_count):
        piece = var_shift(mixed, step) if step else mixed
        place = (var_place - step) % var_count
        every_token = lax.dynamic_update_slice_in_dim(every_token, piece, place * part_tokens, 0)
    product = jnp.dot(every_token, out_weight, preferred_element_type=f32)
    product = product.astype(jnp.bfloat16).reshape(tok_rows, mp_count, -1).transpose(1, 0, 2)
    terms = lax.all_to_all(product, "mp", split_axis=0, concat_axis=0, tiled=True)
    summed = terms.astype(f32).sum(0)
    return (summed + out_bias.astype(f32)[None, :]).astype(jnp.bfloat16)


def solution(mesh):
    in_specs = (
        P("var", "tok", None),
        P("var", None, "mp"),
        P("var", "mp"),
        P("tok", "mp"),
        P("tok", None),
        P(None, "var", "mp"),
        P(None, "var", "mp"),
        P("mp", "var"),
        P(("var", "mp")),
    )
    out_specs = P("tok", ("var", "mp"))
    return jax.shard_map(
        on_device, mesh=mesh, in_specs=in_specs, out_specs=out_specs, check_vma=False
    )
```

time: 182 us -> 140 us (0.77)
  waiting for transfers between devices: 108 us -> 41.2 us
  starting transfers between devices: 13.4 us -> 51 us
  blocking collectives: 20.5 us -> 0 us
  Pallas kernels: 0 us -> 13.5 us
  between operations: 13.5 us -> 0.45 us
  local copies, waits for them, and re-layouts: 2.41 us -> 12.2 us
  other arithmetic: 7.26 us -> 2.76 us
    all_gather x1 -> x0, waiting for transfers between devices: 72.8 us -> none  [on_device(): gathered = lax.all_gather(block, 'mp', axis=0, tiled=True)]
    ppermute x0 -> x29, starting transfers between devices: none -> 40.5 us  [the longest x23 29.7 us: move(): return lax.ppermute(array, 'mp', pairs)]
    ppermute x0 -> x29, waiting for transfers between devices: none -> 32.6 us  [the longest x23 22.9 us: move(): return lax.ppermute(array, 'mp', pairs)]
    all_to_all x1, waiting for transfers between devices: 26.2 us -> 0.01 us  [on_device(): lax.all_to_all(own, 'var', split_axis=0, concat_axis=0, tiled=True)]
    pallas_call x0 -> x10, Pallas kernels: none -> 13.5 us  [the longest x4 7.09 us: line_of(): pl.pallas_call(functools.partial(line_kernel, chunk), in_specs=[pl.BlockS...]
    all_to_all x1 -> x0, blocking collectives: 11.4 us -> none  [on_device(): lax.all_to_all(own, 'var', split_axis=0, concat_axis=3, tiled=True)]
    unnamed x8 -> x34, local copies, waits for them, and re-layouts: 0.02 us -> 9.33 us
    all_gather x1 -> x0, blocking collectives: 9.03 us -> none  [on_device(): every_token = lax.all_gather(mixed, 'var', axis=0, tiled=True)]
  transfers between devices with their start and end apart: 3 -> 31, of which waited for: 3 -> 12; matrix products, arithmetic and copies ran while one was open for 0% -> 11% of each run, Pallas kernels for 0% -> 8%
where the time goes in v2:
time: 140 us; the launch traced here: 139 us
  starting transfers between devices  51 us (36%)
  waiting for transfers between devices  41.2 us (29%)
  matrix products  17.6 us (13%)
  Pallas kernels  13.5 us (10%)
  local copies, waits for them, and re-layouts  12.2 us (9%)
  other arithmetic  2.76 us (2%)
    ppermute x23, starting transfers between devices, move(): return lax.ppermute(array, 'mp', pairs)  29.7 us
    ppermute x23, waiting for transfers between devices, move(): return lax.ppermute(array, 'mp', pairs)  22.9 us
    dot_general x20, matrix products, product(): total = total + jnp.dot(part, weight, preferred_element_type=f32)  14.1 us
    ppermute x5, waiting for transfers between devices, var_shift(): return lax.ppermute(array, 'var', [(k, (k + step) % n) for k in range(n)])  9.64 us
    unnamed x34, local copies, waits for them, and re-layouts  9.33 us
    all_to_all x1, waiting for transfers between devices, on_device(): lax.all_to_all(product, 'mp', split_axis=0, concat_axis=0, tiled=True)  8.65 us
    ppermute x5, starting transfers between devices, var_shift(): return lax.ppermute(array, 'var', [(k, (k + step) % n) for k in range(n)])  8.06 us
    pallas_call x4, Pallas kernels, line_of(): pl.pallas_call(functools.partial(line_kernel, chunk), in_specs=[pl.BlockS...  7.09 us
  transfers between devices with their start and end apart: 31, of which 12 were waited for; matrix products, arithmetic and copies ran while one was open for 11% of the time, Pallas kernels for 8%

profile of v2, /device:TPU:1, one launch (start us, length us, event | category | flops | bytes accessed | tf_op | source)
XLA Modules:
  0.0 138.7 jit_solution(5515305369004095468)
XLA Ops:
  0.9 1.6 %fusion.15 = bf16[22,16,384]{2,1,0:T(8,128)(2,1)S(1)} fusion(bf16[22,16,64]{2,1,0:T(8,128)(2,1)} %param.11, bf16[22,64,384]{2,1,0:T(8,128)(2,1)} %param.12, f32[22,384]{1,0:T(8,128)S(1)} %convert_element_type.41), kind=kOutput, calls=%fused_computation.28 | convolution fusion | flops 17571840 | bytes 1430528 | tf_op jit(solution)/shard_map/vtp,vpc->vtc/dot_general | solution.py:217
  3.6 4.8 %all-to-all-start = ((bf16[4,4,88,96]{3,2,1,0:T(8,128)(2,1)}), bf16[4,4,88,96]{3,2,1,0:T(8,128)(2,1)S(1)}, u32[]{:S(2)}, u32[]{:S(2)}) async-start(bf16[4,4,88,96]{3,2,1,0:T(8,128)(2,1)} %bitcast.6), calls=%async_computation | async-start | bytes 720896 | tf_op jit(solution)/shard_map/all_to_all | solution.py:224
  9.1 1.7 %copy-done.9 = bf16[32,96,384]{2,1,0:T(8,128)(2,1)S(1)} copy-done((bf16[32,96,384]{2,1,0:T(8,128)(2,1)S(1)}, bf16[32,96,384]{2,1,0:T(8,128)(2,1)}, u32[]{:S(2)}) %copy-start.9) | copy-done | bytes 2359320
  10.8 1.7 %copy-done.10 = bf16[32,96,384]{2,1,0:T(8,128)(2,1)S(1)} copy-done((bf16[32,96,384]{2,1,0:T(8,128)(2,1)S(1)}, bf16[32,96,384]{2,1,0:T(8,128)(2,1)}, u32[]{:S(2)}) %copy-start.10) | copy-done | bytes 2359320
  12.5 4.2 %order_weights.1 = (bf16[8,96,768]{2,1,0:T(8,128)(2,1)}, bf16[8,96,768]{2,1,0:T(8,128)(2,1)}, bf16[8,96,768]{2,1,0:T(8,128)(2,1)}, bf16[4,96,768]{2,1,0:T(8,128)(2,1)}, bf16[4,96,768]{2,1,0:T(8,128)(2,1)}) custom-call(s32[32]{0:T(128)S(1)} %fusion.28.order, bf16[32,96,384]{2,1,0:T(8,128)(2,1)S(1)} %copy-done.9, bf16[32,96,384]{2,1,0:T(8,128)(2,1)S(1)} %copy-done.10), custom_call_target="tpu_custom_call" | custom-call | bytes 10485760 | tf_op jit(solution)/shard_map/order_weights/pallas_call | solution.py:145
  18.1 1.7 %collective-permute-start = (bf16[4,88,384]{2,1,0:T(8,128)(2,1)S(1)}, bf16[4,88,384]{2,1,0:T(8,128)(2,1)S(1)}, u32[]{:S(2)}, u32[]{:S(2)}) collective-permute-start(bf16[4,88,384]{2,1,0:T(8,128)(2,1)S(1)} %pack.1.refs_0_), channel_id=1, source_target_pairs={{0,8},{1,9},{2,10},{3,11},{4,12},{5,13},{6,14},{7,15},{8,16},{9,17... | collective-permute-start | bytes 811016 | tf_op jit(solution)/shard_map/ppermute | solution.py:26
  19.8 2.8 %collective-permute-start.1 = (bf16[4,88,384]{2,1,0:T(8,128)(2,1)S(1)}, bf16[4,88,384]{2,1,0:T(8,128)(2,1)S(1)}, u32[]{:S(2)}, u32[]{:S(2)}) collective-permute-start(bf16[4,88,384]{2,1,0:T(8,128)(2,1)S(1)} %pack.1.refs_0_), channel_id=1, source_target_pairs={{0,24},{1,25},{2,26},{3,27},{4,28},{5,29},{6,30},{7,31},{8,0},{9,1... | collective-permute-start | bytes 811016 | tf_op jit(solution)/shard_map/ppermute | solution.py:26
  22.8 1.6 %collective-permute-start.3 = (bf16[4,88,384]{2,1,0:T(8,128)(2,1)S(1)}, bf16[4,88,384]{2,1,0:T(8,128)(2,1)}, u32[]{:S(2)}, u32[]{:S(2)}) collective-permute-start(bf16[4,88,384]{2,1,0:T(8,128)(2,1)S(1)} %pack.1.refs_0_), channel_id=1, source_target_pairs={{0,1},{1,0},{2,3},{3,2},{4,5},{5,4},{6,7},{7,6},{8,9},{9,8},{10,11... | collective-permute-start | bytes 811016 | tf_op jit(solution)/shard_map/ppermute | solution.py:26
  24.5 3.9 %collective-permute-done.refs_1_ = bf16[4,88,384]{2,1,0:T(8,128)(2,1)S(1)} collective-permute-done((bf16[4,88,384]{2,1,0:T(8,128)(2,1)S(1)}, bf16[4,88,384]{2,1,0:T(8,128)(2,1)S(1)}, u32[]{:S(2)}, u32[]{:S(2)}) %collective-permute-start) | collective-permute-done | bytes 270368 | tf_op jit(solution)/shard_map/ppermute | solution.py:26
  28.4 3.0 %collective-permute-start.4 = (bf16[4,88,384]{2,1,0:T(8,128)(2,1)S(1)}, bf16[4,88,384]{2,1,0:T(8,128)(2,1)}, u32[]{:S(2)}, u32[]{:S(2)}) collective-permute-start(bf16[4,88,384]{2,1,0:T(8,128)(2,1)S(1)} %collective-permute-done.refs_1_), channel_id=1, source_target_pairs={{0,1},{1,0},{2,3},{3,2},{4,5},{5,4},{6,7},{7,6},{8,9},{9,8},{10,11... | collective-permute-start | bytes 811016 | tf_op jit(solution)/shard_map/ppermute | solution.py:26
  31.3 1.8 %collective-permute-done.1.refs_2_ = bf16[4,88,384]{2,1,0:T(8,128)(2,1)S(1)} collective-permute-done((bf16[4,88,384]{2,1,0:T(8,128)(2,1)S(1)}, bf16[4,88,384]{2,1,0:T(8,128)(2,1)S(1)}, u32[]{:S(2)}, u32[]{:S(2)}) %collective-permute-start.1) | collective-permute-done | bytes 270368 | tf_op jit(solution)/shard_map/ppermute | solution.py:26
  33.1 1.6 %collective-permute-start.5 = (bf16[4,88,384]{2,1,0:T(8,128)(2,1)S(1)}, bf16[4,88,384]{2,1,0:T(8,128)(2,1)}, u32[]{:S(2)}, u32[]{:S(2)}) collective-permute-start(bf16[4,88,384]{2,1,0:T(8,128)(2,1)S(1)} %collective-permute-done.1.refs_2_), channel_id=1, source_target_pairs={{0,1},{1,0},{2,3},{3,2},{4,5},{5,4},{6,7},{7,6},{8,9},{9,8},{10,11... | collective-permute-start | bytes 811016 | tf_op jit(solution)/shard_map/ppermute | solution.py:26
  35.4 11.4 %collective-permute-done.2.refs_3_ = bf16[4,88,384]{2,1,0:T(8,128)(2,1)S(1)} collective-permute-done((bf16[4,88,384]{2,1,0:T(8,128)(2,1)S(1)}, bf16[4,88,384]{2,1,0:T(8,128)(2,1)S(1)}, u32[]{:S(2)}, u32[]{:S(2)}) %collective-permute-start.2) | collective-permute-done | bytes 270368 | tf_op jit(solution)/shard_map/ppermute | solution.py:26
  52.1 2.8 %collective-permute-start.7 = (bf16[352,768]{1,0:T(8,128)(2,1)S(1)}, bf16[352,768]{1,0:T(8,128)(2,1)}, u32[]{:S(2)}, u32[]{:S(2)}) collective-permute-start(bf16[352,768]{1,0:T(8,128)(2,1)S(1)} %line.4.after), channel_id=1, source_target_pairs={{0,2},{1,7},{2,4},{3,1},{4,6},{5,3},{6,0},{7,5},{8,10},{9,15},{10,... | collective-permute-start | bytes 1622024 | tf_op jit(solution)/shard_map/ppermute | solution.py:26
  55.0 2.4 %line.5.after = bf16[352,768]{1,0:T(8,128)(2,1)} custom-call(s32[4]{0:T(128)S(1)} %pad_add_fusion.groups, bf16[352,768]{1,0:T(8,128)(2,1)S(1)} %line.4.after, bf16[4,88,384]{2,1,0:T(8,128)(2,1)S(1)} %pack.1.refs_0_, bf16[4,88,384]{2,1,0:T(8,128)(2,1)S(1)} %collective-permute-done.refs_1_, bf16[4,88,384]{2,1,0:T(8,128)(2,1)S(1)} %copy-done.4, ...), custom_call_target="tpu_custom_call" | custom-call | bytes 65536 | tf_op jit(solution)/shard_map/line/pallas_call | solution.py:103
  58.7 2.5 %collective-permute-done.7.array = bf16[352,768]{1,0:T(8,128)(2,1)} collective-permute-done((bf16[352,768]{1,0:T(8,128)(2,1)S(1)}, bf16[352,768]{1,0:T(8,128)(2,1)}, u32[]{:S(2)}, u32[]{:S(2)}) %collective-permute-start.7) | collective-permute-done | bytes 540704 | tf_op jit(solution)/shard_map/ppermute | solution.py:26
  62.2 3.3 %collective-permute-start.13 = (bf16[352,384]{1,0:T(8,128)(2,1)S(1)}, bf16[352,384]{1,0:T(8,128)(2,1)S(1)}, u32[]{:S(2)}, u32[]{:S(2)}) collective-permute-start(bf16[352,384]{1,0:T(8,128)(2,1)S(1)} %half.4.after), channel_id=1, source_target_pairs={{0,2},{1,7},{2,4},{3,1},{4,6},{5,3},{6,0},{7,5},{8,10},{9,15},{10,... | collective-permute-start | bytes 811016 | tf_op jit(solution)/shard_map/ppermute | solution.py:26
  67.2 1.6 %line.7 = bf16[352,768]{1,0:T(8,128)(2,1)S(1)} custom-call(s32[4]{0:T(128)S(1)} %pad_add_fusion.groups, bf16[352,768]{1,0:T(8,128)(2,1)S(1)} %line.6.after, bf16[4,88,384]{2,1,0:T(8,128)(2,1)S(1)} %pack.1.refs_0_, bf16[4,88,384]{2,1,0:T(8,128)(2,1)S(1)} %collective-permute-done.refs_1_, bf16[4,88,384]{2,1,0:T(8,128)(2,1)S(1)} %copy-done.5, ...), custom_call_target="tpu_custom_call" | custom-call | bytes 65536 | tf_op jit(solution)/shard_map/line/pallas_call | solution.py:103
  68.9 1.9 %collective-permute-start.12 = (bf16[352,768]{1,0:T(8,128)(2,1)}, bf16[352,768]{1,0:T(8,128)(2,1)S(1)}, u32[]{:S(2)}, u32[]{:S(2)}) collective-permute-start(bf16[352,768]{1,0:T(8,128)(2,1)} %collective-permute-done.7.array), channel_id=1, source_target_pairs={{0,1},{1,0},{2,3},{3,2},{4,5},{5,4},{6,7},{7,6},{8,9},{9,8},{10,11... | collective-permute-start | bytes 1622024 | tf_op jit(solution)/shard_map/ppermute | solution.py:26
  70.8 1.6 %fusion.34 = f32[352,768]{1,0:T(8,128)S(1)} fusion(bf16[352,768]{1,0:T(8,128)(2,1)} %collective-permute-done.7.array, bf16[768,768]{1,0:T(8,128)(2,1)S(1)} %bitcast.72), kind=kOutput, calls=%fused_computation.62 | convolution fusion | flops 415236096 | bytes 2801664 | tf_op jit(solution)/shard_map/dot_general | solution.py:239
  72.6 1.7 %fusion.32 = f32[352,768]{1,0:T(8,128)S(1)} fusion(bf16[352,768]{1,0:T(8,128)(2,1)} %collective-permute-done.10.array, bf16[768,768]{1,0:T(8,128)(2,1)S(1)} %bitcast.73), kind=kOutput, calls=%fused_computation.60 | convolution fusion | flops 415236096 | bytes 2801664 | tf_op jit(solution)/shard_map/dot_general | solution.py:239
  78.4 2.8 %collective-permute-start.17 = (bf16[352,768]{1,0:T(8,128)(2,1)S(1)}, bf16[352,768]{1,0:T(8,128)(2,1)S(1)}, u32[]{:S(2)}, u32[]{:S(2)}) collective-permute-start(bf16[352,768]{1,0:T(8,128)(2,1)S(1)} %fusion.14.after), channel_id=1, source_target_pairs={{0,64},{1,193},{2,66},{3,195},{4,68},{5,197},{6,70},{7,199},{8,72}... | collective-permute-start | bytes 1622024 | tf_op jit(solution)/shard_map/ppermute | solution.py:188
  82.1 1.8 %collective-permute-start.15 = (bf16[352,384]{1,0:T(8,128)(2,1)S(1)}, bf16[352,384]{1,0:T(8,128)(2,1)S(1)}, u32[]{:S(2)}, u32[]{:S(2)}) collective-permute-start(bf16[352,384]{1,0:T(8,128)(2,1)S(1)} %half.5.after), channel_id=1, source_target_pairs={{0,2},{1,7},{2,4},{3,1},{4,6},{5,3},{6,0},{7,5},{8,10},{9,15},{10,... | collective-permute-start | bytes 811016 | tf_op jit(solution)/shard_map/ppermute | solution.py:26
  87.8 1.6 %collective-permute-start.16 = (bf16[352,384]{1,0:T(8,128)(2,1)S(1)}, bf16[352,384]{1,0:T(8,128)(2,1)S(1)}, u32[]{:S(2)}, u32[]{:S(2)}) collective-permute-start(bf16[352,384]{1,0:T(8,128)(2,1)S(1)} %collective-permute-done.15), channel_id=1, source_target_pairs={{0,1},{1,0},{2,3},{3,2},{4,5},{5,4},{6,7},{7,6},{8,9},{9,8},{10,11... | collective-permute-start | bytes 811016 | tf_op jit(solution)/shard_map/ppermute | solution.py:26
  90.7 1.6 %collective-permute-start.24 = (bf16[352,384]{1,0:T(8,128)(2,1)S(1)}, bf16[352,384]{1,0:T(8,128)(2,1)S(1)}, u32[]{:S(2)}, u32[]{:S(2)}) collective-permute-start(bf16[352,384]{1,0:T(8,128)(2,1)S(1)} %collective-permute-done.23), channel_id=1, source_target_pairs={{0,1},{1,0},{2,3},{3,2},{4,5},{5,4},{6,7},{7,6},{8,9},{9,8},{10,11... | collective-permute-start | bytes 811016 | tf_op jit(solution)/shard_map/ppermute | solution.py:26
  92.3 1.7 %fusion.9 = f32[352,768]{1,0:T(8,128)S(1)} fusion(f32[352,768]{1,0:T(8,128)S(1)} %fusion.37, f32[352,768]{1,0:T(8,128)S(1)} %fusion.33, f32[352,768]{1,0:T(8,128)S(1)} %fusion.32, bf16[352,768]{1,0:T(8,128)(2,1)} %line.5.after, bf16[768,768]{1,0:T(8,128)(2,1)S(1)} %bitcast.65), kind=kOutput, calls=%fused_computation.17 | convolution fusion | flops 416047104 | bytes 6045696 | tf_op jit(solution)/shard_map/dot_general | solution.py:239
  98.7 2.1 %collective-permute-start.25 = (bf16[352,768]{1,0:T(8,128)(2,1)S(1)}, bf16[352,768]{1,0:T(8,128)(2,1)S(1)}, u32[]{:S(2)}, u32[]{:S(2)}) collective-permute-start(bf16[352,768]{1,0:T(8,128)(2,1)S(1)} %fusion.13), channel_id=1, source_target_pairs={{0,192},{64,0},{128,64},{192,128},{1,193},{65,1},{129,65},{193,129... | collective-permute-start | bytes 1622024 | tf_op jit(solution)/shard_map/ppermute | solution.py:193
  102.1 2.3 %collective-permute-start.19 = (bf16[352,384]{1,0:T(8,128)(2,1)S(1)}, bf16[352,384]{1,0:T(8,128)(2,1)S(1)}, u32[]{:S(2)}, u32[]{:S(2)}) collective-permute-start(bf16[352,384]{1,0:T(8,128)(2,1)S(1)} %collective-permute-done.18), channel_id=1, source_target_pairs={{0,1},{1,0},{2,3},{3,2},{4,5},{5,4},{6,7},{7,6},{8,9},{9,8},{10,11... | collective-permute-start | bytes 811016 | tf_op jit(solution)/shard_map/ppermute | solution.py:26
  105.6 7.2 %collective-permute-done.25 = bf16[352,768]{1,0:T(8,128)(2,1)S(1)} collective-permute-done((bf16[352,768]{1,0:T(8,128)(2,1)S(1)}, bf16[352,768]{1,0:T(8,128)(2,1)S(1)}, u32[]{:S(2)}, u32[]{:S(2)}) %collective-permute-start.25) | collective-permute-done | bytes 540704 | tf_op jit(solution)/shard_map/ppermute | solution.py:193
  116.1 3.9 %collective-permute-start.27 = (bf16[4,384]{1,0:T(4,128)(2,1)S(1)}, bf16[4,384]{1,0:T(4,128)(2,1)S(1)}, u32[]{:S(2)}, u32[]{:S(2)}) collective-permute-start(bf16[4,384]{1,0:T(4,128)(2,1)S(1)} %get-tuple-element.36), channel_id=1, source_target_pairs={{0,128},{64,192},{128,0},{192,64},{1,129},{65,193},{129,1},{193,65... | collective-permute-start | bytes 9224 | tf_op jit(solution)/shard_map/ppermute | solution.py:193
  123.8 5.6 %all-to-all-start.1 = ((bf16[32,16,96]{2,1,0:T(8,128)(2,1)}), bf16[32,16,96]{2,1,0:T(8,128)(2,1)S(1)}, u32[]{:S(2)}, u32[]{:S(2)}) async-start(bf16[32,16,96]{2,1,0:T(8,128)(2,1)} %bitcast.63), calls=%async_computation.1 | async-start | bytes 262144 | tf_op jit(solution)/shard_map/all_to_all | solution.py:287
  129.4 8.6 %all-to-all-done.1 = bf16[32,16,96]{2,1,0:T(8,128)(2,1)S(1)} async-done(((bf16[32,16,96]{2,1,0:T(8,128)(2,1)}), bf16[32,16,96]{2,1,0:T(8,128)(2,1)S(1)}, u32[]{:S(2)}, u32[]{:S(2)}) %all-to-all-start.1) | async-done | bytes 98336 | tf_op jit(solution)/shard_map/all_to_all | solution.py:287
  (119 shorter events, 39.4 us)
Async XLA Ops:
  0.0 122.5 %copy-start = (bf16[384,3072]{1,0:T(8,128)(2,1)S(1)}, bf16[384,3072]{1,0:T(8,128)(2,1)}, u32[]{:S(2)}) copy-start(bf16[384,3072]{1,0:T(8,128)(2,1)} %param.18) | copy-start | bytes 7077892
  3.6 13.1 %all-to-all-start = ((bf16[4,4,88,96]{3,2,1,0:T(8,128)(2,1)}), bf16[4,4,88,96]{3,2,1,0:T(8,128)(2,1)S(1)}, u32[]{:S(2)}, u32[]{:S(2)}) async-start(bf16[4,4,88,96]{3,2,1,0:T(8,128)(2,1)} %bitcast.6), calls=%async_computation | async-start | bytes 720896 | tf_op jit(solution)/shard_map/all_to_all | solution.py:224
  18.1 10.2 %collective-permute-start = (bf16[4,88,384]{2,1,0:T(8,128)(2,1)S(1)}, bf16[4,88,384]{2,1,0:T(8,128)(2,1)S(1)}, u32[]{:S(2)}, u32[]{:S(2)}) collective-permute-start(bf16[4,88,384]{2,1,0:T(8,128)(2,1)S(1)} %pack.1.refs_0_), channel_id=1, source_target_pairs={{0,8},{1,9},{2,10},{3,11},{4,12},{5,13},{6,14},{7,15},{8,16},{9,17... | collective-permute-start | bytes 811016 | tf_op jit(solution)/shard_map/ppermute | solution.py:26
  19.8 13.2 %collective-permute-start.1 = (bf16[4,88,384]{2,1,0:T(8,128)(2,1)S(1)}, bf16[4,88,384]{2,1,0:T(8,128)(2,1)S(1)}, u32[]{:S(2)}, u32[]{:S(2)}) collective-permute-start(bf16[4,88,384]{2,1,0:T(8,128)(2,1)S(1)} %pack.1.refs_0_), channel_id=1, source_target_pairs={{0,24},{1,25},{2,26},{3,27},{4,28},{5,29},{6,30},{7,31},{8,0},{9,1... | collective-permute-start | bytes 811016 | tf_op jit(solution)/shard_map/ppermute | solution.py:26
  22.6 24.2 %collective-permute-start.2 = (bf16[4,88,384]{2,1,0:T(8,128)(2,1)S(1)}, bf16[4,88,384]{2,1,0:T(8,128)(2,1)S(1)}, u32[]{:S(2)}, u32[]{:S(2)}) collective-permute-start(bf16[4,88,384]{2,1,0:T(8,128)(2,1)S(1)} %pack.1.refs_0_), channel_id=1, source_target_pairs={{0,16},{1,17},{2,18},{3,19},{4,20},{5,21},{6,22},{7,23},{8,24},{9,... | collective-permute-start | bytes 811016 | tf_op jit(solution)/shard_map/ppermute | solution.py:26
  22.8 25.3 %collective-permute-start.3 = (bf16[4,88,384]{2,1,0:T(8,128)(2,1)S(1)}, bf16[4,88,384]{2,1,0:T(8,128)(2,1)}, u32[]{:S(2)}, u32[]{:S(2)}) collective-permute-start(bf16[4,88,384]{2,1,0:T(8,128)(2,1)S(1)} %pack.1.refs_0_), channel_id=1, source_target_pairs={{0,1},{1,0},{2,3},{3,2},{4,5},{5,4},{6,7},{7,6},{8,9},{9,8},{10,11... | collective-permute-start | bytes 811016 | tf_op jit(solution)/shard_map/ppermute | solution.py:26
  28.4 19.8 %collective-permute-start.4 = (bf16[4,88,384]{2,1,0:T(8,128)(2,1)S(1)}, bf16[4,88,384]{2,1,0:T(8,128)(2,1)}, u32[]{:S(2)}, u32[]{:S(2)}) collective-permute-start(bf16[4,88,384]{2,1,0:T(8,128)(2,1)S(1)} %collective-permute-done.refs_1_), channel_id=1, source_target_pairs={{0,1},{1,0},{2,3},{3,2},{4,5},{5,4},{6,7},{7,6},{8,9},{9,8},{10,11... | collective-permute-start | bytes 811016 | tf_op jit(solution)/shard_map/ppermute | solution.py:26
  33.1 15.1 %collective-permute-start.5 = (bf16[4,88,384]{2,1,0:T(8,128)(2,1)S(1)}, bf16[4,88,384]{2,1,0:T(8,128)(2,1)}, u32[]{:S(2)}, u32[]{:S(2)}) collective-permute-start(bf16[4,88,384]{2,1,0:T(8,128)(2,1)S(1)} %collective-permute-done.1.refs_2_), channel_id=1, source_target_pairs={{0,1},{1,0},{2,3},{3,2},{4,5},{5,4},{6,7},{7,6},{8,9},{9,8},{10,11... | collective-permute-start | bytes 811016 | tf_op jit(solution)/shard_map/ppermute | solution.py:26
  46.9 1.8 %collective-permute-start.6 = (bf16[4,88,384]{2,1,0:T(8,128)(2,1)S(1)}, bf16[4,88,384]{2,1,0:T(8,128)(2,1)}, u32[]{:S(2)}, u32[]{:S(2)}) collective-permute-start(bf16[4,88,384]{2,1,0:T(8,128)(2,1)S(1)} %collective-permute-done.2.refs_3_), channel_id=1, source_target_pairs={{0,1},{1,0},{2,3},{3,2},{4,5},{5,4},{6,7},{7,6},{8,9},{9,8},{10,11... | collective-permute-start | bytes 811016 | tf_op jit(solution)/shard_map/ppermute | solution.py:26
  52.1 9.1 %collective-permute-start.7 = (bf16[352,768]{1,0:T(8,128)(2,1)S(1)}, bf16[352,768]{1,0:T(8,128)(2,1)}, u32[]{:S(2)}, u32[]{:S(2)}) collective-permute-start(bf16[352,768]{1,0:T(8,128)(2,1)S(1)} %line.4.after), channel_id=1, source_target_pairs={{0,2},{1,7},{2,4},{3,1},{4,6},{5,3},{6,0},{7,5},{8,10},{9,15},{10,... | collective-permute-start | bytes 1622024 | tf_op jit(solution)/shard_map/ppermute | solution.py:26
  57.3 15.2 %collective-permute-start.10 = (bf16[352,768]{1,0:T(8,128)(2,1)}, bf16[352,768]{1,0:T(8,128)(2,1)}, u32[]{:S(2)}, u32[]{:S(2)}) collective-permute-start(bf16[352,768]{1,0:T(8,128)(2,1)} %line.5.after), channel_id=1, source_target_pairs={{0,2},{1,7},{2,4},{3,1},{4,6},{5,3},{6,0},{7,5},{8,10},{9,15},{10,... | collective-permute-start | bytes 1622024 | tf_op jit(solution)/shard_map/ppermute | solution.py:26
  62.2 12.1 %collective-permute-start.13 = (bf16[352,384]{1,0:T(8,128)(2,1)S(1)}, bf16[352,384]{1,0:T(8,128)(2,1)S(1)}, u32[]{:S(2)}, u32[]{:S(2)}) collective-permute-start(bf16[352,384]{1,0:T(8,128)(2,1)S(1)} %half.4.after), channel_id=1, source_target_pairs={{0,2},{1,7},{2,4},{3,1},{4,6},{5,3},{6,0},{7,5},{8,10},{9,15},{10,... | collective-permute-start | bytes 811016 | tf_op jit(solution)/shard_map/ppermute | solution.py:26
  67.1 16.8 %collective-permute-start.21 = (bf16[352,768]{1,0:T(8,128)(2,1)S(1)}, bf16[352,768]{1,0:T(8,128)(2,1)S(1)}, u32[]{:S(2)}, u32[]{:S(2)}) collective-permute-start(bf16[352,768]{1,0:T(8,128)(2,1)S(1)} %line.6.after), channel_id=1, source_target_pairs={{0,2},{1,7},{2,4},{3,1},{4,6},{5,3},{6,0},{7,5},{8,10},{9,15},{10,... | collective-permute-start | bytes 1622024 | tf_op jit(solution)/shard_map/ppermute | solution.py:26
  68.8 15.4 %collective-permute-start.8 = (bf16[352,768]{1,0:T(8,128)(2,1)S(1)}, bf16[352,768]{1,0:T(8,128)(2,1)S(1)}, u32[]{:S(2)}, u32[]{:S(2)}) collective-permute-start(bf16[352,768]{1,0:T(8,128)(2,1)S(1)} %line.7), channel_id=1, source_target_pairs={{0,2},{1,7},{2,4},{3,1},{4,6},{5,3},{6,0},{7,5},{8,10},{9,15},{10,... | collective-permute-start | bytes 1622024 | tf_op jit(solution)/shard_map/ppermute | solution.py:26
  68.9 6.4 %collective-permute-start.12 = (bf16[352,768]{1,0:T(8,128)(2,1)}, bf16[352,768]{1,0:T(8,128)(2,1)S(1)}, u32[]{:S(2)}, u32[]{:S(2)}) collective-permute-start(bf16[352,768]{1,0:T(8,128)(2,1)} %collective-permute-done.7.array), channel_id=1, source_target_pairs={{0,1},{1,0},{2,3},{3,2},{4,5},{5,4},{6,7},{7,6},{8,9},{9,8},{10,11... | collective-permute-start | bytes 1622024 | tf_op jit(solution)/shard_map/ppermute | solution.py:26
  72.5 13.0 %collective-permute-start.11 = (bf16[352,768]{1,0:T(8,128)(2,1)}, bf16[352,768]{1,0:T(8,128)(2,1)S(1)}, u32[]{:S(2)}, u32[]{:S(2)}) collective-permute-start(bf16[352,768]{1,0:T(8,128)(2,1)} %collective-permute-done.10.array), channel_id=1, source_target_pairs={{0,1},{1,0},{2,3},{3,2},{4,5},{5,4},{6,7},{7,6},{8,9},{9,8},{10,11... | collective-permute-start | bytes 1622024 | tf_op jit(solution)/shard_map/ppermute | solution.py:26
  74.3 3.2 %collective-permute-start.14 = (bf16[352,384]{1,0:T(8,128)(2,1)S(1)}, bf16[352,384]{1,0:T(8,128)(2,1)S(1)}, u32[]{:S(2)}, u32[]{:S(2)}) collective-permute-start(bf16[352,384]{1,0:T(8,128)(2,1)S(1)} %collective-permute-done.13), channel_id=1, source_target_pairs={{0,1},{1,0},{2,3},{3,2},{4,5},{5,4},{6,7},{7,6},{8,9},{9,8},{10,11... | collective-permute-start | bytes 811016 | tf_op jit(solution)/shard_map/ppermute | solution.py:26
  78.4 16.0 %collective-permute-start.17 = (bf16[352,768]{1,0:T(8,128)(2,1)S(1)}, bf16[352,768]{1,0:T(8,128)(2,1)S(1)}, u32[]{:S(2)}, u32[]{:S(2)}) collective-permute-start(bf16[352,768]{1,0:T(8,128)(2,1)S(1)} %fusion.14.after), channel_id=1, source_target_pairs={{0,64},{1,193},{2,66},{3,195},{4,68},{5,197},{6,70},{7,199},{8,72}... | collective-permute-start | bytes 1622024 | tf_op jit(solution)/shard_map/ppermute | solution.py:188
  82.1 5.7 %collective-permute-start.15 = (bf16[352,384]{1,0:T(8,128)(2,1)S(1)}, bf16[352,384]{1,0:T(8,128)(2,1)S(1)}, u32[]{:S(2)}, u32[]{:S(2)}) collective-permute-start(bf16[352,384]{1,0:T(8,128)(2,1)S(1)} %half.5.after), channel_id=1, source_target_pairs={{0,2},{1,7},{2,4},{3,1},{4,6},{5,3},{6,0},{7,5},{8,10},{9,15},{10,... | collective-permute-start | bytes 811016 | tf_op jit(solution)/shard_map/ppermute | solution.py:26
  83.9 6.8 %collective-permute-start.23 = (bf16[352,384]{1,0:T(8,128)(2,1)S(1)}, bf16[352,384]{1,0:T(8,128)(2,1)S(1)}, u32[]{:S(2)}, u32[]{:S(2)}) collective-permute-start(bf16[352,384]{1,0:T(8,128)(2,1)S(1)} %half.7), channel_id=1, source_target_pairs={{0,2},{1,7},{2,4},{3,1},{4,6},{5,3},{6,0},{7,5},{8,10},{9,15},{10,... | collective-permute-start | bytes 811016 | tf_op jit(solution)/shard_map/ppermute | solution.py:26
  84.3 16.5 %collective-permute-start.9 = (bf16[352,768]{1,0:T(8,128)(2,1)S(1)}, bf16[352,768]{1,0:T(8,128)(2,1)S(1)}, u32[]{:S(2)}, u32[]{:S(2)}) collective-permute-start(bf16[352,768]{1,0:T(8,128)(2,1)S(1)} %collective-permute-done.8.array), channel_id=1, source_target_pairs={{0,1},{1,0},{2,3},{3,2},{4,5},{5,4},{6,7},{7,6},{8,9},{9,8},{10,11... | collective-permute-start | bytes 1622024 | tf_op jit(solution)/shard_map/ppermute | solution.py:26
  85.5 11.5 %collective-permute-start.22 = (bf16[352,768]{1,0:T(8,128)(2,1)S(1)}, bf16[352,768]{1,0:T(8,128)(2,1)S(1)}, u32[]{:S(2)}, u32[]{:S(2)}) collective-permute-start(bf16[352,768]{1,0:T(8,128)(2,1)S(1)} %collective-permute-done.21.array), channel_id=1, source_target_pairs={{0,1},{1,0},{2,3},{3,2},{4,5},{5,4},{6,7},{7,6},{8,9},{9,8},{10,11... | collective-permute-start | bytes 1622024 | tf_op jit(solution)/shard_map/ppermute | solution.py:26
  87.8 6.6 %collective-permute-start.16 = (bf16[352,384]{1,0:T(8,128)(2,1)S(1)}, bf16[352,384]{1,0:T(8,128)(2,1)S(1)}, u32[]{:S(2)}, u32[]{:S(2)}) collective-permute-start(bf16[352,384]{1,0:T(8,128)(2,1)S(1)} %collective-permute-done.15), channel_id=1, source_target_pairs={{0,1},{1,0},{2,3},{3,2},{4,5},{5,4},{6,7},{7,6},{8,9},{9,8},{10,11... | collective-permute-start | bytes 811016 | tf_op jit(solution)/shard_map/ppermute | solution.py:26
  90.7 7.5 %collective-permute-start.24 = (bf16[352,384]{1,0:T(8,128)(2,1)S(1)}, bf16[352,384]{1,0:T(8,128)(2,1)S(1)}, u32[]{:S(2)}, u32[]{:S(2)}) collective-permute-start(bf16[352,384]{1,0:T(8,128)(2,1)S(1)} %collective-permute-done.23), channel_id=1, source_target_pairs={{0,1},{1,0},{2,3},{3,2},{4,5},{5,4},{6,7},{7,6},{8,9},{9,8},{10,11... | collective-permute-start | bytes 811016 | tf_op jit(solution)/shard_map/ppermute | solution.py:26
  94.9 18.0 %collective-permute-start.20 = (bf16[352,768]{1,0:T(8,128)(2,1)S(1)}, bf16[352,768]{1,0:T(8,128)(2,1)S(1)}, u32[]{:S(2)}, u32[]{:S(2)}) collective-permute-start(bf16[352,768]{1,0:T(8,128)(2,1)S(1)} %fusion.12.after), channel_id=1, source_target_pairs={{0,64},{64,128},{128,192},{192,0},{1,65},{65,129},{129,193},{193,1... | collective-permute-start | bytes 1622024 | tf_op jit(solution)/shard_map/ppermute | solution.py:193
  96.2 5.9 %collective-permute-start.18 = (bf16[352,384]{1,0:T(8,128)(2,1)S(1)}, bf16[352,384]{1,0:T(8,128)(2,1)S(1)}, u32[]{:S(2)}, u32[]{:S(2)}) collective-permute-start(bf16[352,384]{1,0:T(8,128)(2,1)S(1)} %half.6), channel_id=1, source_target_pairs={{0,2},{1,7},{2,4},{3,1},{4,6},{5,3},{6,0},{7,5},{8,10},{9,15},{10,... | collective-permute-start | bytes 811016 | tf_op jit(solution)/shard_map/ppermute | solution.py:26
  98.7 14.2 %collective-permute-start.25 = (bf16[352,768]{1,0:T(8,128)(2,1)S(1)}, bf16[352,768]{1,0:T(8,128)(2,1)S(1)}, u32[]{:S(2)}, u32[]{:S(2)}) collective-permute-start(bf16[352,768]{1,0:T(8,128)(2,1)S(1)} %fusion.13), channel_id=1, source_target_pairs={{0,192},{64,0},{128,64},{192,128},{1,193},{65,1},{129,65},{193,129... | collective-permute-start | bytes 1622024 | tf_op jit(solution)/shard_map/ppermute | solution.py:193
  102.1 3.5 %collective-permute-start.19 = (bf16[352,384]{1,0:T(8,128)(2,1)S(1)}, bf16[352,384]{1,0:T(8,128)(2,1)S(1)}, u32[]{:S(2)}, u32[]{:S(2)}) collective-permute-start(bf16[352,384]{1,0:T(8,128)(2,1)S(1)} %collective-permute-done.18), channel_id=1, source_target_pairs={{0,1},{1,0},{2,3},{3,2},{4,5},{5,4},{6,7},{7,6},{8,9},{9,8},{10,11... | collective-permute-start | bytes 811016 | tf_op jit(solution)/shard_map/ppermute | solution.py:26
  115.3 4.7 %collective-permute-start.26 = (bf16[4,384]{1,0:T(4,128)(2,1)S(1)}, bf16[4,384]{1,0:T(4,128)(2,1)S(1)}, u32[]{:S(2)}, u32[]{:S(2)}) collective-permute-start(bf16[4,384]{1,0:T(4,128)(2,1)S(1)} %get-tuple-element.36), channel_id=1, source_target_pairs={{0,64},{64,128},{128,192},{192,0},{1,65},{65,129},{129,193},{193,1... | collective-permute-start | bytes 9224 | tf_op jit(solution)/shard_map/ppermute | solution.py:193
  116.1 4.9 %collective-permute-start.27 = (bf16[4,384]{1,0:T(4,128)(2,1)S(1)}, bf16[4,384]{1,0:T(4,128)(2,1)S(1)}, u32[]{:S(2)}, u32[]{:S(2)}) collective-permute-start(bf16[4,384]{1,0:T(4,128)(2,1)S(1)} %get-tuple-element.36), channel_id=1, source_target_pairs={{0,128},{64,192},{128,0},{192,64},{1,129},{65,193},{129,1},{193,65... | collective-permute-start | bytes 9224 | tf_op jit(solution)/shard_map/ppermute | solution.py:193
  120.0 2.4 %collective-permute-start.28 = (bf16[4,384]{1,0:T(4,128)(2,1)S(1)}, bf16[4,384]{1,0:T(4,128)(2,1)S(1)}, u32[]{:S(2)}, u32[]{:S(2)}) collective-permute-start(bf16[4,384]{1,0:T(4,128)(2,1)S(1)} %get-tuple-element.36), channel_id=1, source_target_pairs={{0,192},{64,0},{128,64},{192,128},{1,193},{65,1},{129,65},{193,129... | collective-permute-start | bytes 9224 | tf_op jit(solution)/shard_map/ppermute | solution.py:193
  123.8 14.3 %all-to-all-start.1 = ((bf16[32,16,96]{2,1,0:T(8,128)(2,1)}), bf16[32,16,96]{2,1,0:T(8,128)(2,1)S(1)}, u32[]{:S(2)}, u32[]{:S(2)}) async-start(bf16[32,16,96]{2,1,0:T(8,128)(2,1)} %bitcast.63), calls=%async_computation.1 | async-start | bytes 262144 | tf_op jit(solution)/shard_map/all_to_all | solution.py:287
  (16 other events, 71.3 us)
